TPU v7x, 32 devices: a whole 2x2x4 slice. The times are simulated.
32 devices in a mesh: groups: 2 (over x), visit: 16 (over z, y, core).
Axes of the slice: x: 2, y: 2, z: 4, core: 2. Of those that a mesh axis runs over, the one named last changes fastest.
Arguments:
- science: float32 [8192, 1024], P(('groups', 'visit')), parts along dimension 0, may hold values from -6 to 6
- template: bfloat16 [8192, 1024], P(('groups', 'visit')), parts along dimension 0, may hold values from -6 to 6
- owner_map: int32 [32], P('groups'), parts along dimension 0, may hold values from 0 to 15, as said below
- covering: int32 [32, 4], P(('groups', 'visit')), parts along dimension 0, may hold values from 0 to 15, as said below
- row_shift: int32 [32, 4], P(('groups', 'visit')), parts along dimension 0, may hold values from -128 to 128, as said below
- col_shift: int32 [32, 4], P(('groups', 'visit')), parts along dimension 0, may hold values from -256 to 256, as said below
- basis_cols: float32 [20, 21], replicated, may hold values from -1.25 to 1.25
- basis_rows: float32 [20, 21], replicated, may hold values from -1.25 to 1.25
- coeffs: float32 [8, 20], P('groups'), parts along dimension 0, may hold values from -1.25 to 1.25
- psf_kernel: float32 [9, 9], replicated, may hold values from 0 to 0.25
Outputs:
- difference: float32 [8192, 1024], P(('groups', 'visit')), parts along dimension 0
- detection: float32 [8192, 1024], P(('groups', 'visit')), parts along dimension 0
There are 2 independent parts, one for each index of `groups`. A program takes and returns all parts, laid end to end along the dimension named above; an argument that names none is the same for every part. Nothing has to cross between parts.
Inputs may be any that keep to these rules, and one draw needn't show every extreme that they name: owner_map is a permutation: every device stores exactly one template piece. `covering`: the 4 pieces listed for a row block are different; the first is the piece stored on that block's own device; every listed piece is stored on a device at most 3 positions away along the visit axis, and on some device exactly 3. `row_shift`: the first slot of every row block has shift 0; both ends of the range are reached. `col_shift`: the first slot of every row block has shift 0; both ends of the range are reached.
All inputs are finite; a program needn't handle non-finite values.
Results may differ from a plain program's by a relative error of at most 0.005.
Values may be sent and summed in bfloat16 or wider, within the bound.
A program may use at most 64 MiB of HBM per device.

v0:
```python
import functools

import jax
import jax.numpy as jnp
from jax import lax
from jax.experimental import pallas as pl
from jax.experimental.pallas import tpu as pltpu
from jax.sharding import PartitionSpec as P

PIECES = 4
REACH = 3
LANES = 128
EDGE = 16
MESH = pl.DeviceIdType.MESH


def kernel(
    devices,
    owner_ref,
    covering_ref,
    row_shift_ref,
    col_shift_ref,
    science_ref,
    template_ref,
    basis_cols_ref,
    basis_rows_ref,
    coeffs_ref,
    psf_ref,
    difference_ref,
    detection_ref,
    slots,
    ext,
    ext_low,
    sci_ext,
    small,
    folded,
    weights,
    psf_weights,
    y_model,
    y_psf,
    diff_ext,
    diff_low,
    partial,
    partials,
    piece_send,
    piece_recv,
    forward_send,
    sci_send,
    sci_recv,
    halo_send,
    halo_recv,
    part_send,
    part_recv,
):
    rows, cols = science_ref.shape
    blocks = cols // LANES
    taps = basis_cols_ref.shape[1]
    basis = basis_cols_ref.shape[0]
    psf_taps = psf_ref.shape[0]
    rim, psf_rim = taps // 2, psf_taps // 2
    f32, bf16 = jnp.float32, jnp.bfloat16

    group = lax.axis_index("groups")
    me = lax.axis_index("visit")
    core = lax.rem(me, 2)
    sibling = me + 1 - 2 * core
    held = lax.rem(me + 1, devices)
    visit = held // PIECES
    pos = lax.rem(held, PIECES)
    before = lax.rem(me + devices - 1, devices)
    after = lax.rem(me + 1, devices)
    far = jnp.where(core == 1, me + REACH, me - REACH)
    has_low, has_high = me >= 2, me + 2 < devices
    has_far = (far >= 0) & (far < devices)
    has_before, has_after = pos > 0, pos < PIECES - 1

    def peer(step):
        return lax.rem(visit * PIECES + lax.rem(pos + step, PIECES) + devices - 1, devices)

    barrier = pltpu.get_barrier_semaphore()

    def greet(device):
        pl.semaphore_signal(barrier, inc=1, device_id=(group, device), device_id_type=MESH)

    greet(sibling)
    for step in range(1, PIECES):
        greet(peer(step))
    pl.when(has_low)(lambda: greet(me - 2))
    pl.when(has_high)(lambda: greet(me + 2))
    pl.when(has_far)(lambda: greet(far))
    expected = (
        PIECES + has_low.astype(jnp.int32) + has_high.astype(jnp.int32) + has_far.astype(jnp.int32)
    )
    pl.semaphore_wait(barrier, expected)

    def remote(src, dst, send, recv, device):
        return pltpu.make_async_remote_copy(
            src_ref=src,
            dst_ref=dst,
            send_sem=send,
            recv_sem=recv,
            device_id=(group, device),
            device_id_type=MESH,
        )

    def piece_copy(src, slot, send, device):
        return remote(src, slots.at[slot], send, piece_recv.at[slot], device)

    far_slot = jnp.where(core == 1, 0, 2 * REACH)
    to_high = piece_copy(template_ref, 1, piece_send.at[0], me + 2)
    to_low = piece_copy(template_ref, 5, piece_send.at[1], me - 2)
    to_far = piece_copy(template_ref, far_slot, piece_send.at[2], far)
    to_sibling = piece_copy(template_ref, 2 + 2 * core, piece_send.at[3], sibling)
    sci_up = remote(
        science_ref.at[pl.ds(0, 8)], sci_ext.at[pl.ds(8 + rows, 8)], sci_send.at[0], sci_recv.at[1], before
    )
    sci_down = remote(
        science_ref.at[pl.ds(rows - 8, 8)], sci_ext.at[pl.ds(0, 8)], sci_send.at[1], sci_recv.at[0], after
    )
    pl.when(has_high)(to_high.start)
    pl.when(has_low)(to_low.start)
    pl.when(has_far)(to_far.start)
    to_sibling.start()
    pl.when(has_before)(sci_up.start)
    pl.when(has_after)(sci_down.start)

    lane = lax.broadcasted_iota(jnp.int32, (LANES, 2 * LANES), 1)
    tap = lax.broadcasted_iota(jnp.int32, (LANES, 2 * LANES), 0)
    reverse = jnp.where(lax.rem(tap + lane, 2 * LANES) == 0, 1.0, 0.0).astype(bf16)
    small[...] = jnp.zeros_like(small)
    small[0, 0:basis, 0:taps] = basis_cols_ref[...]
    small[1, 0:basis, 0:taps] = basis_rows_ref[...]
    small[2, 0:psf_taps, 0:psf_taps] = psf_ref[...]
    small[3, 0:1, 0:basis] = coeffs_ref[pl.ds(visit, 1), :]
    diagonal = lax.broadcasted_iota(jnp.int32, (LANES, LANES), 0) == lax.broadcasted_iota(
        jnp.int32, (LANES, LANES), 1
    )
    coeff_col = jnp.sum(
        jnp.where(diagonal, jnp.broadcast_to(small[3, 0:1, :], (LANES, LANES)), 0.0),
        axis=1,
        keepdims=True,
    )
    row_weights = (coeff_col * small[1]).astype(bf16).astype(f32)
    cols_reversed = jnp.dot(small[0].astype(bf16), reverse, preferred_element_type=f32)
    folded[0] = jnp.dot(
        row_weights.T.astype(bf16), cols_reversed.astype(bf16), preferred_element_type=f32
    )
    folded[1] = jnp.dot(small[2].astype(bf16), reverse, preferred_element_type=f32)

    def band(which, index):
        line = folded[which, pl.ds(index, 1), :]
        spread = jnp.broadcast_to(line, (2 * LANES, 2 * LANES))
        rolled = pltpu.roll(spread, 0, 1, stride=1, stride_axis=0)
        return rolled[:, :LANES].astype(bf16)

    steps = (taps + 7) // 8

    def build(step, carry):
        start = pl.multiple_of(step * (2 * LANES), 2 * LANES)
        for s in range(8):
            weights[pl.ds(start, 2 * LANES), s * LANES : (s + 1) * LANES] = band(0, step * 8 + s)
        return carry

    lax.fori_loop(0, steps, build, 0)
    for s in range(psf_taps):
        psf_weights[:, s * LANES : (s + 1) * LANES] = band(1, s)

    sci_ext[pl.ds(8, rows), :] = science_ref[...]
    sci_ext[pl.ds(rows + 16, 8), :] = jnp.zeros((8, cols), f32)
    ext[pl.ds(rows + 2 * EDGE, EDGE), :] = jnp.zeros((EDGE, ext.shape[1]), bf16)
    slots[REACH] = template_ref[...]

    @pl.when(jnp.logical_not(has_before))
    def _():
        sci_ext[pl.ds(0, 8), :] = jnp.zeros((8, cols), f32)
        ext[pl.ds(0, EDGE), :] = jnp.zeros((EDGE, ext.shape[1]), bf16)

    @pl.when(jnp.logical_not(has_after))
    def _():
        sci_ext[pl.ds(rows + 8, 8), :] = jnp.zeros((8, cols), f32)
        ext[pl.ds(rows + EDGE, EDGE), :] = jnp.zeros((EDGE, ext.shape[1]), bf16)

    from_low = piece_copy(slots.at[1], 2 * core, forward_send.at[0], sibling)
    from_high = piece_copy(slots.at[5], 4 + 2 * core, forward_send.at[1], sibling)

    @pl.when(has_low)
    def _():
        piece_copy(template_ref, 1, piece_send.at[0], sibling).wait_recv()
        from_low.start()

    @pl.when(has_high)
    def _():
        piece_copy(template_ref, 5, piece_send.at[0], sibling).wait_recv()
        from_high.start()

    for slot in (0, 2, 4, 6):
        origin = me + slot - REACH
        pl.when((origin >= 0) & (origin < devices))(
            piece_copy(template_ref, slot, piece_send.at[0], sibling).wait_recv
        )

    row_to = lax.broadcasted_iota(jnp.int32, (rows, rows), 0)
    row_from = lax.broadcasted_iota(jnp.int32, (rows, rows), 1)
    row_line = lax.broadcasted_iota(jnp.int32, (rows, cols), 0)
    col_line = lax.broadcasted_iota(jnp.int32, (rows, cols), 1)
    total = template_ref[...].astype(f32)
    coverage = jnp.ones((rows, cols), f32)
    for k in range(1, covering_ref.shape[1]):
        holder = owner_ref[covering_ref[0, k]]
        row_off, col_off = row_shift_ref[0, k], col_shift_ref[0, k]
        piece = slots[jnp.clip(holder - me + REACH, 0, 2 * REACH)]
        select = jnp.where(row_to - row_from == row_off, 1.0, 0.0).astype(bf16)
        moved = jnp.dot(select, piece, preferred_element_type=f32)
        moved = pltpu.roll(moved, lax.rem(col_off + cols, cols), 1)
        col_old, row_old = col_line - col_off, row_line - row_off
        col_in = (col_old >= 0) & (col_old < cols)
        total = total + jnp.where(col_in, moved, 0.0)
        coverage = coverage + jnp.where(col_in & (row_old >= 0) & (row_old < rows), 1.0, 0.0)
    canvas = total / coverage
    wide = jnp.concatenate([canvas, jnp.zeros((rows, LANES), f32)], axis=1)
    ext[pl.ds(EDGE, rows), :] = pltpu.roll(wide, rim, 1).astype(bf16)

    halo_up = remote(
        ext.at[pl.ds(EDGE, EDGE)], ext.at[pl.ds(rows + EDGE, EDGE)], halo_send.at[0], halo_recv.at[1], before
    )
    halo_down = remote(
        ext.at[pl.ds(rows, EDGE)], ext.at[pl.ds(0, EDGE)], halo_send.at[1], halo_recv.at[0], after
    )
    pl.when(has_before)(halo_up.start)
    pl.when(has_after)(halo_down.start)

    @pl.when(has_before)
    def _():
        halo_down.wait_recv()
        sci_down.wait_recv()

    @pl.when(has_after)
    def _():
        halo_up.wait_recv()
        sci_up.wait_recv()

    ext_low[...] = ext[...].astype(f32)[8 : rows + 2 * EDGE + 8].astype(bf16)
    model_rows = rows + 2 * EDGE
    wide_rows = rows + EDGE
    index = lax.broadcasted_iota(jnp.int32, (wide_rows, LANES), 0)
    low_edge = jnp.where(has_before, 0, psf_rim)
    high_edge = jnp.where(has_after, rows + 2 * psf_rim, rows + psf_rim)
    inside = (index >= low_edge) & (index < high_edge)

    def model_block(block, squares):
        start = pl.multiple_of(block * LANES, LANES)
        window = pl.ds(start, 2 * LANES)
        parts = []
        for step in range(steps):
            if step % 2 == 0:
                parts.append(ext[pl.ds(8 * step, model_rows), window])
            else:
                parts.append(ext_low[pl.ds(8 * (step - 1), model_rows), window])
        product = jnp.dot(
            jnp.concatenate(parts, axis=1), weights[...], preferred_element_type=f32
        )
        for s in range(8):
            y_model[s] = product[:, s * LANES : (s + 1) * LANES]
        first = EDGE - rim - psf_rim
        model = y_model[0, pl.ds(first, wide_rows), :]
        for s in range(1, 8):
            model = model + y_model[s, pl.ds(first + s, wide_rows), :]
        diff = sci_ext[pl.ds(8 - psf_rim, wide_rows), pl.ds(start, LANES)] - model
        diff = jnp.where(inside, diff, 0.0)
        diff_ext[:, pl.ds(start, LANES)] = diff
        own = diff[psf_rim : psf_rim + rows]
        difference_ref[:, pl.ds(start, LANES)] = own
        return squares + jnp.sum((own * own).reshape(rows // 8, 8, LANES), axis=0)

    partial[...] = lax.fori_loop(0, blocks, model_block, jnp.zeros((8, LANES), f32))
    part_copies = []
    for step in range(1, PIECES):
        part_copies.append(
            remote(partial, partials.at[pos], part_send.at[step - 1], part_recv.at[pos], peer(step))
        )
    for copy in part_copies:
        copy.start()
    partials[pos] = partial[...]

    tail = jnp.zeros((wide_rows, LANES), f32)
    diff_low[...] = pltpu.roll(jnp.concatenate([diff_ext[...], tail], axis=1), psf_rim, 1).astype(bf16)

    def psf_block(block, carry):
        start = pl.multiple_of(block * LANES, LANES)
        product = jnp.dot(
            diff_low[:, pl.ds(start, 2 * LANES)], psf_weights[...], preferred_element_type=f32
        )
        for s in range(psf_taps):
            y_psf[s] = product[:, s * LANES : (s + 1) * LANES]
        response = y_psf[0, pl.ds(0, rows), :]
        for s in range(1, psf_taps):
            response = response + y_psf[s, pl.ds(s, rows), :]
        detection_ref[:, pl.ds(start, LANES)] = response
        return carry

    lax.fori_loop(0, blocks, psf_block, 0)

    for step in range(1, PIECES):
        source = lax.rem(pos + step, PIECES)
        remote(
            partial, partials.at[source], part_send.at[step - 1], part_recv.at[source], peer(step)
        ).wait_recv()
    variance = jnp.sum(jnp.sum(partials[...], axis=0), keepdims=True) / (PIECES * rows * cols)
    detection_ref[...] = detection_ref[...] / jnp.sqrt(variance + 1e-06)

    pl.when(has_high)(to_high.wait_send)
    pl.when(has_low)(to_low.wait_send)
    pl.when(has_far)(to_far.wait_send)
    to_sibling.wait_send()
    pl.when(has_low)(from_low.wait_send)
    pl.when(has_high)(from_high.wait_send)
    pl.when(has_before)(sci_up.wait_send)
    pl.when(has_after)(sci_down.wait_send)
    pl.when(has_before)(halo_up.wait_send)
    pl.when(has_after)(halo_down.wait_send)
    for copy in part_copies:
        copy.wait_send()


def shards(
    science,
    template,
    owner_map,
    covering,
    row_shift,
    col_shift,
    basis_cols,
    basis_rows,
    coeffs,
    psf_kernel,
):
    rows, cols = science.shape
    devices = lax.axis_size("visit")
    steps = (basis_cols.shape[1] + 7) // 8
    psf_taps = psf_kernel.shape[0]
    f32, bf16 = jnp.float32, jnp.bfloat16
    smem = pl.BlockSpec(memory_space=pltpu.SMEM)
    vmem = pl.BlockSpec(memory_space=pltpu.VMEM)
    wide = cols + LANES
    dma = pltpu.SemaphoreType.DMA
    flops = 2 * cols * (rows + 32) * (2 * LANES) * (8 * steps + psf_taps)
    return pl.pallas_call(
        functools.partial(kernel, devices),
        out_shape=[jax.ShapeDtypeStruct((rows, cols), f32)] * 2,
        in_specs=[smem] * 4 + [vmem] * 6,
        out_specs=[vmem] * 2,
        scratch_shapes=[
            pltpu.VMEM((2 * REACH + 1, rows, cols), bf16),
            pltpu.VMEM((rows + 3 * EDGE, wide), bf16),
            pltpu.VMEM((rows + 2 * EDGE, wide), bf16),
            pltpu.VMEM((rows + 24, cols), f32),
            pltpu.VMEM((4, LANES, LANES), f32),
            pltpu.VMEM((2, LANES, 2 * LANES), f32),
            pltpu.VMEM((steps * 2 * LANES, 8 * LANES), bf16),
            pltpu.VMEM((2 * LANES, psf_taps * LANES), bf16),
            pltpu.VMEM((8, rows + 2 * EDGE, LANES), f32),
            pltpu.VMEM((psf_taps, rows + EDGE, LANES), f32),
            pltpu.VMEM((rows + EDGE, cols), f32),
            pltpu.VMEM((rows + EDGE, wide), bf16),
            pltpu.VMEM((8, LANES), f32),
            pltpu.VMEM((PIECES, 8, LANES), f32),
            dma((4,)),
            dma((2 * REACH + 1,)),
            dma((2,)),
            dma((2,)),
            dma((2,)),
            dma((2,)),
            dma((2,)),
            dma((PIECES - 1,)),
            dma((PIECES,)),
        ],
        compiler_params=pltpu.CompilerParams(
            collective_id=0, has_side_effects=True, vmem_limit_bytes=48 * 1024 * 1024
        ),
        cost_estimate=pl.CostEstimate(
            flops=flops, bytes_accessed=rows * cols * 14, transcendentals=0
        ),
    )(
        owner_map,
        covering,
        row_shift,
        col_shift,
        science,
        template,
        basis_cols,
        basis_rows,
        coeffs,
        psf_kernel,
    )


def solution(mesh):
    return jax.shard_map(
        shards,
        mesh=mesh,
        in_specs=(
            P(("groups", "visit"), None),
            P(("groups", "visit"), None),
            P("groups"),
            P(("groups", "visit"), None),
            P(("groups", "visit"), None),
            P(("groups", "visit"), None),
            P(),
            P(),
            P("groups", None),
            P(),
        ),
        out_specs=(P(("groups", "visit"), None), P(("groups", "visit"), None)),
        check_vma=False,
    )
```

profile of v0, /device:TPU:1, one launch (start us, length us, event | category | flops | bytes accessed | tf_op | source)
XLA Modules:
  0.0 56.2 jit_solution(9026923722851849863)
XLA Ops:
  0.6 0.0 copy-start
  0.6 1.2 %copy-done = f32[256,1024]{1,0:T(8,128)S(1)} copy-done((f32[256,1024]{1,0:T(8,128)S(1)}, f32[256,1024]{1,0:T(8,128)}, u32[]{:S(2)}) %copy-start) | copy-done | bytes 1048600
  1.9 0.0 copy-start.1
  1.9 1.0 %copy-done.1 = bf16[256,1024]{1,0:T(8,128)(2,1)S(1)} copy-done((bf16[256,1024]{1,0:T(8,128)(2,1)S(1)}, bf16[256,1024]{1,0:T(8,128)(2,1)}, u32[]{:S(2)}) %copy-start.1) | copy-done | bytes 524312
  2.9 0.0 copy-start.2
  2.9 0.7 %copy-done.2 = f32[20,21]{1,0:T(8,128)S(1)} copy-done((f32[20,21]{1,0:T(8,128)S(1)}, f32[20,21]{1,0:T(8,128)}, u32[]{:S(2)}) %copy-start.2) | copy-done | bytes 1704
  3.6 0.0 copy-start.3
  3.6 0.7 %copy-done.3 = f32[20,21]{1,0:T(8,128)S(1)} copy-done((f32[20,21]{1,0:T(8,128)S(1)}, f32[20,21]{1,0:T(8,128)}, u32[]{:S(2)}) %copy-start.3) | copy-done | bytes 1704
  4.3 0.0 copy-start.4
  4.3 0.7 %copy-done.4 = f32[9,9]{1,0:T(8,128)S(1)} copy-done((f32[9,9]{1,0:T(8,128)S(1)}, f32[9,9]{1,0:T(8,128)}, u32[]{:S(2)}) %copy-start.4) | copy-done | bytes 348
  5.0 0.0 copy-start.5
  5.0 0.7 %copy-done.5 = f32[4,20]{1,0:T(4,128)S(1)} copy-done((f32[4,20]{1,0:T(4,128)S(1)}, f32[4,20]{1,0:T(4,128)}, u32[]{:S(2)}) %copy-start.5) | copy-done | bytes 344
  5.7 0.0 copy-start.6
  5.7 0.7 %copy-done.6 = s32[16]{0:T(128)S(1)} copy-done((s32[16]{0:T(128)S(1)}, s32[16]{0:T(128)}, u32[]{:S(2)}) %copy-start.6) | copy-done | bytes 88
  6.4 0.0 copy-start.7
  6.4 0.7 %copy-done.7 = s32[1,4]{1,0:T(1,128)S(1)} copy-done((s32[1,4]{1,0:T(1,128)S(1)}, s32[1,4]{1,0:T(1,128)}, u32[]{:S(2)}) %copy-start.7) | copy-done | bytes 40
  7.0 0.0 copy-start.8
  7.0 0.7 %copy-done.8 = s32[1,4]{1,0:T(1,128)S(1)} copy-done((s32[1,4]{1,0:T(1,128)S(1)}, s32[1,4]{1,0:T(1,128)}, u32[]{:S(2)}) %copy-start.8) | copy-done | bytes 40
  7.7 0.0 copy-start.9
  7.7 0.7 %copy-done.9 = s32[1,4]{1,0:T(1,128)S(1)} copy-done((s32[1,4]{1,0:T(1,128)S(1)}, s32[1,4]{1,0:T(1,128)}, u32[]{:S(2)}) %copy-start.9) | copy-done | bytes 40
  8.3 46.0 %shard_map.113 = (f32[256,1024]{1,0:T(8,128)S(1)}, f32[256,1024]{1,0:T(8,128)S(1)}) custom-call(s32[16]{0:T(128)S(1)} %copy-done.6, s32[1,4]{1,0:T(1,128)S(1)} %copy-done.7, s32[1,4]{1,0:T(1,128)S(1)} %copy-done.8, s32[1,4]{1,0:T(1,128)S(1)} %copy-done.9, f32[256,1024]{1,0:T(8,128)S(1)} %copy-done, bf16[256,1024]{1,0:T(8,128)(2,1)S(1)} %copy-done.1, ...), custom_call_target="tpu_custom_call" | custom-call | flops 4982833152 | bytes 3670016 | tf_op jit(solution)/shard_map/pallas_call | solution.py:347
  54.3 1.0 %copy.14 = f32[256,1024]{1,0:T(8,128)} copy(f32[256,1024]{1,0:T(8,128)S(1)} %get-tuple-element.4) | data formatting | bytes 2097152
  55.3 1.0 %copy.15 = f32[256,1024]{1,0:T(8,128)} copy(f32[256,1024]{1,0:T(8,128)S(1)} %get-tuple-element.5) | data formatting | bytes 2097152
Async XLA Ops:
  0.6 1.2 %copy-start = (f32[256,1024]{1,0:T(8,128)S(1)}, f32[256,1024]{1,0:T(8,128)}, u32[]{:S(2)}) copy-start(f32[256,1024]{1,0:T(8,128)} %science_ref.1) | copy-start | bytes 3145732
  1.9 1.0 %copy-start.1 = (bf16[256,1024]{1,0:T(8,128)(2,1)S(1)}, bf16[256,1024]{1,0:T(8,128)(2,1)}, u32[]{:S(2)}) copy-start(bf16[256,1024]{1,0:T(8,128)(2,1)} %template_ref.1) | copy-start | bytes 1572868
  2.9 0.7 %copy-start.2 = (f32[20,21]{1,0:T(8,128)S(1)}, f32[20,21]{1,0:T(8,128)}, u32[]{:S(2)}) copy-start(f32[20,21]{1,0:T(8,128)} %basis_cols_ref.1) | copy-start | bytes 5044
  3.6 0.7 %copy-start.3 = (f32[20,21]{1,0:T(8,128)S(1)}, f32[20,21]{1,0:T(8,128)}, u32[]{:S(2)}) copy-start(f32[20,21]{1,0:T(8,128)} %basis_rows_ref.1) | copy-start | bytes 5044
  4.3 0.7 %copy-start.4 = (f32[9,9]{1,0:T(8,128)S(1)}, f32[9,9]{1,0:T(8,128)}, u32[]{:S(2)}) copy-start(f32[9,9]{1,0:T(8,128)} %psf_ref.1) | copy-start | bytes 976
  5.0 0.7 %copy-start.5 = (f32[4,20]{1,0:T(4,128)S(1)}, f32[4,20]{1,0:T(4,128)}, u32[]{:S(2)}) copy-start(f32[4,20]{1,0:T(4,128)} %coeffs_ref.1) | copy-start | bytes 964
  5.7 0.7 %copy-start.6 = (s32[16]{0:T(128)S(1)}, s32[16]{0:T(128)}, u32[]{:S(2)}) copy-start(s32[16]{0:T(128)} %owner_ref.1) | copy-start | bytes 196
  6.4 0.7 %copy-start.7 = (s32[1,4]{1,0:T(1,128)S(1)}, s32[1,4]{1,0:T(1,128)}, u32[]{:S(2)}) copy-start(s32[1,4]{1,0:T(1,128)} %covering_ref.1) | copy-start | bytes 52
  7.0 0.7 %copy-start.8 = (s32[1,4]{1,0:T(1,128)S(1)}, s32[1,4]{1,0:T(1,128)}, u32[]{:S(2)}) copy-start(s32[1,4]{1,0:T(1,128)} %row_shift_ref.1) | copy-start | bytes 52
  7.7 0.7 %copy-start.9 = (s32[1,4]{1,0:T(1,128)S(1)}, s32[1,4]{1,0:T(1,128)}, u32[]{:S(2)}) copy-start(s32[1,4]{1,0:T(1,128)} %col_shift_ref.1) | copy-start | bytes 52
where the time goes:
time: 56.7 us; the launch traced here: 56.2 us
  Pallas kernels  46 us (81%)
  local copies, waits for them, and re-layouts  9.61 us (17%)
  between operations  0.66 us (1%)
    pallas_call x1, Pallas kernels, shards(): pl.pallas_call(functools.partial(kernel, devices), out_shape=[jax.ShapeDt...  46 us
    unnamed x22, local copies, waits for them, and re-layouts  9.61 us

commit v1 on v0

--- a/solution.py
+++ b/solution.py
@@ -16,19 +16,32 @@
 
 def kernel(
     devices,
+    owner_hbm,
+    covering_hbm,
+    row_shift_hbm,
+    col_shift_hbm,
+    science_ref,
+    template_ref,
+    basis_cols_hbm,
+    basis_rows_hbm,
+    coeffs_hbm,
+    psf_hbm,
+    difference_ref,
+    detection_ref,
     owner_ref,
     covering_ref,
     row_shift_ref,
     col_shift_ref,
-    science_ref,
-    template_ref,
     basis_cols_ref,
     basis_rows_ref,
     coeffs_ref,
     psf_ref,
-    difference_ref,
-    detection_ref,
-    slots,
+    own_piece,
+    slots_0,
+    slots_1,
+    slots_2,
+    slots_3,
+    moved,
     ext,
     ext_low,
     sci_ext,
@@ -42,8 +55,10 @@
     diff_low,
     partial,
     partials,
+    fetch,
     piece_send,
     piece_recv,
+    relay_send,
     forward_send,
     sci_send,
     sci_recv,
@@ -63,14 +78,19 @@
     group = lax.axis_index("groups")
     me = lax.axis_index("visit")
     core = lax.rem(me, 2)
+    odd = lax.rem(me // 2, 2)
     sibling = me + 1 - 2 * core
+    beside = me + 2 - 4 * odd
+    onward = me + 4 - 8 * odd
     held = lax.rem(me + 1, devices)
     visit = held // PIECES
     pos = lax.rem(held, PIECES)
     before = lax.rem(me + devices - 1, devices)
     after = lax.rem(me + 1, devices)
     far = jnp.where(core == 1, me + REACH, me - REACH)
-    has_low, has_high = me >= 2, me + 2 < devices
+    has_onward = (onward >= 0) & (onward < devices)
+    back = me - 4 + 8 * odd
+    has_back = (back >= 0) & (back < devices)
     has_far = (far >= 0) & (far < devices)
     has_before, has_after = pos > 0, pos < PIECES - 1
 
@@ -83,13 +103,37 @@
         pl.semaphore_signal(barrier, inc=1, device_id=(group, device), device_id_type=MESH)
 
     greet(sibling)
+    greet(beside)
     for step in range(1, PIECES):
         greet(peer(step))
-    pl.when(has_low)(lambda: greet(me - 2))
-    pl.when(has_high)(lambda: greet(me + 2))
+    pl.when(has_onward)(lambda: greet(onward))
+    pl.when(has_back)(lambda: greet(back))
     pl.when(has_far)(lambda: greet(far))
+    fetches = [
+        pltpu.make_async_copy(src, dst, fetch.at[number])
+        for number, (src, dst) in enumerate(
+            (
+                (owner_hbm, owner_ref),
+                (covering_hbm, covering_ref),
+                (row_shift_hbm, row_shift_ref),
+                (col_shift_hbm, col_shift_ref),
+                (basis_cols_hbm, basis_cols_ref),
+                (basis_rows_hbm, basis_rows_ref),
+                (coeffs_hbm, coeffs_ref),
+                (psf_hbm, psf_ref),
+                (template_ref, own_piece),
+                (science_ref, sci_ext.at[pl.ds(8, rows)]),
+            )
+        )
+    ]
+    for copy in fetches:
+        copy.start()
     expected = (
-        PIECES + has_low.astype(jnp.int32) + has_high.astype(jnp.int32) + has_far.astype(jnp.int32)
+        PIECES
+        + 1
+        + has_onward.astype(jnp.int32)
+        + has_back.astype(jnp.int32)
+        + has_far.astype(jnp.int32)
     )
     pl.semaphore_wait(barrier, expected)
 
@@ -103,26 +147,50 @@
             device_id_type=MESH,
         )
 
-    def piece_copy(src, slot, send, device):
-        return remote(src, slots.at[slot], send, piece_recv.at[slot], device)
-
+    slots = (slots_0, slots_1, slots_2, slots_3)
+    chunks = len(slots)
+    chunk_cols = cols // chunks
+
+    def piece_copy(src, slot, chunk, send, device):
+        return remote(src, slots[chunk].at[slot], send, piece_recv.at[slot, chunk], device)
+
+    def own_chunk(chunk):
+        return template_ref.at[:, pl.ds(chunk * chunk_cols, chunk_cols)]
+
+    def arrival(slot, chunk):
+        return piece_copy(slots[chunk].at[slot], slot, chunk, piece_send.at[0, chunk], sibling)
+
+    beside_slot = 5 - 4 * odd
+    back_slot = 1 + 4 * odd
     far_slot = jnp.where(core == 1, 0, 2 * REACH)
-    to_high = piece_copy(template_ref, 1, piece_send.at[0], me + 2)
-    to_low = piece_copy(template_ref, 5, piece_send.at[1], me - 2)
-    to_far = piece_copy(template_ref, far_slot, piece_send.at[2], far)
-    to_sibling = piece_copy(template_ref, 2 + 2 * core, piece_send.at[3], sibling)
+    to_beside, to_far, to_sibling, to_onward, from_beside, from_back = [], [], [], [], [], []
+    for chunk in range(chunks):
+        src = own_chunk(chunk)
+        to_beside.append(piece_copy(src, back_slot, chunk, piece_send.at[0, chunk], beside))
+        to_far.append(piece_copy(src, far_slot, chunk, piece_send.at[1, chunk], far))
+        to_sibling.append(piece_copy(src, 2 + 2 * core, chunk, piece_send.at[2, chunk], sibling))
+        beside_chunk, back_chunk = slots[chunk].at[beside_slot], slots[chunk].at[back_slot]
+        to_onward.append(piece_copy(beside_chunk, back_slot, chunk, relay_send.at[chunk], onward))
+        from_beside.append(
+            piece_copy(beside_chunk, beside_slot - 1 + 2 * core, chunk, forward_send.at[0, chunk], sibling)
+        )
+        from_back.append(
+            piece_copy(back_chunk, back_slot - 1 + 2 * core, chunk, forward_send.at[1, chunk], sibling)
+        )
     sci_up = remote(
         science_ref.at[pl.ds(0, 8)], sci_ext.at[pl.ds(8 + rows, 8)], sci_send.at[0], sci_recv.at[1], before
     )
     sci_down = remote(
         science_ref.at[pl.ds(rows - 8, 8)], sci_ext.at[pl.ds(0, 8)], sci_send.at[1], sci_recv.at[0], after
     )
-    pl.when(has_high)(to_high.start)
-    pl.when(has_low)(to_low.start)
-    pl.when(has_far)(to_far.start)
-    to_sibling.start()
+    for chunk in range(chunks):
+        to_beside[chunk].start()
+        pl.when(has_far)(to_far[chunk].start)
+        to_sibling[chunk].start()
     pl.when(has_before)(sci_up.start)
     pl.when(has_after)(sci_down.start)
+    for copy in fetches:
+        copy.wait()
 
     lane = lax.broadcasted_iota(jnp.int32, (LANES, 2 * LANES), 1)
     tap = lax.broadcasted_iota(jnp.int32, (LANES, 2 * LANES), 0)
@@ -165,10 +233,16 @@
     for s in range(psf_taps):
         psf_weights[:, s * LANES : (s + 1) * LANES] = band(1, s)
 
-    sci_ext[pl.ds(8, rows), :] = science_ref[...]
     sci_ext[pl.ds(rows + 16, 8), :] = jnp.zeros((8, cols), f32)
     ext[pl.ds(rows + 2 * EDGE, EDGE), :] = jnp.zeros((EDGE, ext.shape[1]), bf16)
-    slots[REACH] = template_ref[...]
+    pad_blocks = (moved.shape[1] - blocks) // 2
+    margin = pad_blocks * LANES
+    for part in range(pad_blocks):
+        for k in range(moved.shape[0]):
+            moved[k, part] = jnp.zeros((rows, LANES), f32)
+            moved[k, pad_blocks + blocks + part] = jnp.zeros((rows, LANES), f32)
+    for part in range(blocks):
+        moved[0, pad_blocks + part] = own_piece[:, part * LANES : (part + 1) * LANES].astype(f32)
 
     @pl.when(jnp.logical_not(has_before))
     def _():
@@ -180,45 +254,65 @@
         sci_ext[pl.ds(rows + 8, 8), :] = jnp.zeros((8, cols), f32)
         ext[pl.ds(rows + EDGE, EDGE), :] = jnp.zeros((EDGE, ext.shape[1]), bf16)
 
-    from_low = piece_copy(slots.at[1], 2 * core, forward_send.at[0], sibling)
-    from_high = piece_copy(slots.at[5], 4 + 2 * core, forward_send.at[1], sibling)
-
-    @pl.when(has_low)
-    def _():
-        piece_copy(template_ref, 1, piece_send.at[0], sibling).wait_recv()
-        from_low.start()
-
-    @pl.when(has_high)
-    def _():
-        piece_copy(template_ref, 5, piece_send.at[0], sibling).wait_recv()
-        from_high.start()
-
-    for slot in (0, 2, 4, 6):
-        origin = me + slot - REACH
-        pl.when((origin >= 0) & (origin < devices))(
-            piece_copy(template_ref, slot, piece_send.at[0], sibling).wait_recv
-        )
-
+    slot_count = moved.shape[0]
     row_to = lax.broadcasted_iota(jnp.int32, (rows, rows), 0)
     row_from = lax.broadcasted_iota(jnp.int32, (rows, rows), 1)
-    row_line = lax.broadcasted_iota(jnp.int32, (rows, cols), 0)
-    col_line = lax.broadcasted_iota(jnp.int32, (rows, cols), 1)
-    total = template_ref[...].astype(f32)
-    coverage = jnp.ones((rows, cols), f32)
-    for k in range(1, covering_ref.shape[1]):
+    places, row_offs, col_offs, selects = [None], [None], [0], [None]
+    for k in range(1, slot_count):
         holder = owner_ref[covering_ref[0, k]]
-        row_off, col_off = row_shift_ref[0, k], col_shift_ref[0, k]
-        piece = slots[jnp.clip(holder - me + REACH, 0, 2 * REACH)]
-        select = jnp.where(row_to - row_from == row_off, 1.0, 0.0).astype(bf16)
-        moved = jnp.dot(select, piece, preferred_element_type=f32)
-        moved = pltpu.roll(moved, lax.rem(col_off + cols, cols), 1)
-        col_old, row_old = col_line - col_off, row_line - row_off
-        col_in = (col_old >= 0) & (col_old < cols)
-        total = total + jnp.where(col_in, moved, 0.0)
-        coverage = coverage + jnp.where(col_in & (row_old >= 0) & (row_old < rows), 1.0, 0.0)
-    canvas = total / coverage
-    wide = jnp.concatenate([canvas, jnp.zeros((rows, LANES), f32)], axis=1)
-    ext[pl.ds(EDGE, rows), :] = pltpu.roll(wide, rim, 1).astype(bf16)
+        places.append(jnp.clip(holder - me + REACH, 0, 2 * REACH))
+        row_offs.append(row_shift_ref[0, k])
+        col_offs.append(col_shift_ref[0, k])
+        selects.append(jnp.where(row_to - row_from == row_offs[k], 1.0, 0.0).astype(bf16))
+
+    def pass_on(chunk):
+        arrival(beside_slot, chunk).wait_recv()
+        pl.when(has_onward)(to_onward[chunk].start)
+        from_beside[chunk].start()
+
+    def canvas_block(start, width):
+        col = lax.broadcasted_iota(jnp.int32, (1, width), 1) + (start - rim)
+        row = lax.broadcasted_iota(jnp.int32, (rows, width), 0)
+        total, coverage = None, jnp.ones((rows, width), f32)
+        for k in range(slot_count):
+            first = margin + start - rim - col_offs[k]
+            base = first // LANES if k == 0 else lax.div(first, LANES)
+            span = width // LANES + 1
+            window = jnp.concatenate([moved[k, base + part] for part in range(span)], axis=1)
+            turn = lax.rem(span * LANES - (first - base * LANES), span * LANES)
+            placed = pltpu.roll(window, turn, 1)[:, :width]
+            total = placed if k == 0 else total + placed
+            if k:
+                col_old, row_old = col - col_offs[k], row - row_offs[k]
+                col_in = jnp.where((col_old >= 0) & (col_old < cols), 1.0, 0.0)
+                row_in = jnp.where((row_old >= 0) & (row_old < rows), 1.0, 0.0)
+                coverage = coverage + row_in * col_in
+        image = jnp.where((col >= 0) & (col < cols), total / coverage, 0.0)
+        ext[pl.ds(EDGE, rows), start : start + width] = image.astype(bf16)
+
+    pass_on(0)
+    for chunk in range(chunks):
+        if chunk + 1 < chunks:
+            pass_on(chunk + 1)
+
+        @pl.when(has_back)
+        def _():
+            arrival(back_slot, chunk).wait_recv()
+            from_back[chunk].start()
+
+        for slot in (0, 2, 4, 6):
+            origin = me + slot - REACH
+            pl.when((origin >= 0) & (origin < devices))(arrival(slot, chunk).wait_recv)
+        for k in range(1, slot_count):
+            product = jnp.dot(selects[k], slots[chunk][places[k]], preferred_element_type=f32)
+            for part in range(chunk_cols // LANES):
+                moved[k, pad_blocks + chunk * (chunk_cols // LANES) + part] = product[
+                    :, part * LANES : (part + 1) * LANES
+                ]
+        if chunk:
+            canvas_block((chunk - 1) * chunk_cols, chunk_cols)
+    canvas_block(cols - chunk_cols, chunk_cols)
+    canvas_block(cols, LANES)
 
     halo_up = remote(
         ext.at[pl.ds(EDGE, EDGE)], ext.at[pl.ds(rows + EDGE, EDGE)], halo_send.at[0], halo_recv.at[1], before
@@ -308,12 +402,13 @@
     variance = jnp.sum(jnp.sum(partials[...], axis=0), keepdims=True) / (PIECES * rows * cols)
     detection_ref[...] = detection_ref[...] / jnp.sqrt(variance + 1e-06)
 
-    pl.when(has_high)(to_high.wait_send)
-    pl.when(has_low)(to_low.wait_send)
-    pl.when(has_far)(to_far.wait_send)
-    to_sibling.wait_send()
-    pl.when(has_low)(from_low.wait_send)
-    pl.when(has_high)(from_high.wait_send)
+    for chunk in range(chunks):
+        to_beside[chunk].wait_send()
+        pl.when(has_far)(to_far[chunk].wait_send)
+        to_sibling[chunk].wait_send()
+        pl.when(has_onward)(to_onward[chunk].wait_send)
+        from_beside[chunk].wait_send()
+        pl.when(has_back)(from_back[chunk].wait_send)
     pl.when(has_before)(sci_up.wait_send)
     pl.when(has_after)(sci_down.wait_send)
     pl.when(has_before)(halo_up.wait_send)
@@ -339,7 +434,9 @@
     steps = (basis_cols.shape[1] + 7) // 8
     psf_taps = psf_kernel.shape[0]
     f32, bf16 = jnp.float32, jnp.bfloat16
-    smem = pl.BlockSpec(memory_space=pltpu.SMEM)
+    hbm = pl.BlockSpec(memory_space=pl.ANY)
+    chunks = 4
+    slot_count = covering.shape[1]
     vmem = pl.BlockSpec(memory_space=pltpu.VMEM)
     wide = cols + LANES
     dma = pltpu.SemaphoreType.DMA
@@ -347,10 +444,20 @@
     return pl.pallas_call(
         functools.partial(kernel, devices),
         out_shape=[jax.ShapeDtypeStruct((rows, cols), f32)] * 2,
-        in_specs=[smem] * 4 + [vmem] * 6,
+        in_specs=[hbm] * 10,
         out_specs=[vmem] * 2,
         scratch_shapes=[
-            pltpu.VMEM((2 * REACH + 1, rows, cols), bf16),
+            pltpu.SMEM(owner_map.shape, jnp.int32),
+            pltpu.SMEM(covering.shape, jnp.int32),
+            pltpu.SMEM(row_shift.shape, jnp.int32),
+            pltpu.SMEM(col_shift.shape, jnp.int32),
+            pltpu.VMEM(basis_cols.shape, f32),
+            pltpu.VMEM(basis_rows.shape, f32),
+            pltpu.VMEM(coeffs.shape, f32),
+            pltpu.VMEM(psf_kernel.shape, f32),
+            pltpu.VMEM((rows, cols), bf16),
+            *([pltpu.VMEM((2 * REACH + 1, rows, cols // chunks), bf16)] * chunks),
+            pltpu.VMEM((slot_count, cols // LANES + 6, rows, LANES), f32),
             pltpu.VMEM((rows + 3 * EDGE, wide), bf16),
             pltpu.VMEM((rows + 2 * EDGE, wide), bf16),
             pltpu.VMEM((rows + 24, cols), f32),
@@ -364,9 +471,11 @@
             pltpu.VMEM((rows + EDGE, wide), bf16),
             pltpu.VMEM((8, LANES), f32),
             pltpu.VMEM((PIECES, 8, LANES), f32),
-            dma((4,)),
-            dma((2 * REACH + 1,)),
-            dma((2,)),
+            dma((10,)),
+            dma((3, chunks)),
+            dma((2 * REACH + 1, chunks)),
+            dma((chunks,)),
+            dma((2, chunks)),
             dma((2,)),
             dma((2,)),
             dma((2,)),
@@ -375,7 +484,7 @@
             dma((PIECES,)),
         ],
         compiler_params=pltpu.CompilerParams(
-            collective_id=0, has_side_effects=True, vmem_limit_bytes=48 * 1024 * 1024
+            collective_id=0, has_side_effects=True, vmem_limit_bytes=60 * 1024 * 1024
         ),
         cost_estimate=pl.CostEstimate(
             flops=flops, bytes_accessed=rows * cols * 14, transcendentals=0

time: 56.7 us -> 46 us (0.81)
  local copies, waits for them, and re-layouts: 9.61 us -> 3.37 us
  Pallas kernels: 46 us -> 41.9 us
    unnamed x22 -> x4, local copies, waits for them, and re-layouts: 9.61 us -> 3.37 us
    pallas_call x1, Pallas kernels: 46 us -> 41.9 us  [shards(): pl.pallas_call(functools.partial(kernel, devices), out_shape=[jax.ShapeDt...]
where the time goes in v1:
time: 46 us; the launch traced here: 45.9 us
  Pallas kernels  41.9 us (91%)
  local copies, waits for them, and re-layouts  3.37 us (7%)
  between operations  0.65 us (1%)
    pallas_call x1, Pallas kernels, shards(): pl.pallas_call(functools.partial(kernel, devices), out_shape=[jax.ShapeDt...  41.9 us
    unnamed x4, local copies, waits for them, and re-layouts  3.37 us

profile of v1, /device:TPU:1, one launch (start us, length us, event | category | flops | bytes accessed | tf_op | source)
XLA Modules:
  0.0 45.9 jit_solution(12749765647869426307)
XLA Ops:
  0.6 41.9 %shard_map.113 = (f32[256,1024]{1,0:T(8,128)}, f32[256,1024]{1,0:T(8,128)}) custom-call(s32[16]{0:T(128)} %owner_hbm.1, s32[1,4]{1,0:T(1,128)} %covering_hbm.1, s32[1,4]{1,0:T(1,128)} %row_shift_hbm.1, s32[1,4]{1,0:T(1,128)} %col_shift_hbm.1, f32[256,1024]{1,0:T(8,128)} %science_ref.1, bf16[256,1024]{1,0:T(8,128)(2,1)} %template_ref.1, ...), custom_call_target="tpu_custom_call" | custom-call | flops 4982833152 | bytes 3670016 | tf_op jit(solution)/shard_map/pallas_call | solution.py:444
  42.5 0.0 copy-start
  42.5 2.4 %copy.14 = f32[256,1024]{1,0:T(8,128)} copy(f32[256,1024]{1,0:T(8,128)} %get-tuple-element.4) | data formatting | bytes 2097152
  44.9 0.0 copy-done
  44.9 1.0 %copy.15 = f32[256,1024]{1,0:T(8,128)} copy(f32[256,1024]{1,0:T(8,128)S(1)} %copy-done) | data formatting | bytes 2097152
Async XLA Ops:
  42.5 2.4 %copy-start = (f32[256,1024]{1,0:T(8,128)S(1)}, f32[256,1024]{1,0:T(8,128)}, u32[]{:S(2)}) copy-start(f32[256,1024]{1,0:T(8,128)} %get-tuple-element.5) | copy-start | bytes 3145732

commit v2 on v1

--- a/solution.py
+++ b/solution.py
@@ -41,6 +41,10 @@
     slots_1,
     slots_2,
     slots_3,
+    slots_4,
+    slots_5,
+    slots_6,
+    slots_7,
     moved,
     ext,
     ext_low,
@@ -147,7 +151,7 @@
             device_id_type=MESH,
         )
 
-    slots = (slots_0, slots_1, slots_2, slots_3)
+    slots = (slots_0, slots_1, slots_2, slots_3, slots_4, slots_5, slots_6, slots_7)
     chunks = len(slots)
     chunk_cols = cols // chunks
 
@@ -290,50 +294,37 @@
         image = jnp.where((col >= 0) & (col < cols), total / coverage, 0.0)
         ext[pl.ds(EDGE, rows), start : start + width] = image.astype(bf16)
 
-    pass_on(0)
-    for chunk in range(chunks):
-        if chunk + 1 < chunks:
-            pass_on(chunk + 1)
-
-        @pl.when(has_back)
-        def _():
-            arrival(back_slot, chunk).wait_recv()
-            from_back[chunk].start()
-
-        for slot in (0, 2, 4, 6):
-            origin = me + slot - REACH
-            pl.when((origin >= 0) & (origin < devices))(arrival(slot, chunk).wait_recv)
-        for k in range(1, slot_count):
-            product = jnp.dot(selects[k], slots[chunk][places[k]], preferred_element_type=f32)
-            for part in range(chunk_cols // LANES):
-                moved[k, pad_blocks + chunk * (chunk_cols // LANES) + part] = product[
-                    :, part * LANES : (part + 1) * LANES
-                ]
-        if chunk:
-            canvas_block((chunk - 1) * chunk_cols, chunk_cols)
-    canvas_block(cols - chunk_cols, chunk_cols)
-    canvas_block(cols, LANES)
-
-    halo_up = remote(
-        ext.at[pl.ds(EDGE, EDGE)], ext.at[pl.ds(rows + EDGE, EDGE)], halo_send.at[0], halo_recv.at[1], before
-    )
-    halo_down = remote(
-        ext.at[pl.ds(rows, EDGE)], ext.at[pl.ds(0, EDGE)], halo_send.at[1], halo_recv.at[0], after
-    )
-    pl.when(has_before)(halo_up.start)
-    pl.when(has_after)(halo_down.start)
-
-    @pl.when(has_before)
-    def _():
-        halo_down.wait_recv()
-        sci_down.wait_recv()
-
-    @pl.when(has_after)
-    def _():
-        halo_up.wait_recv()
-        sci_up.wait_recv()
-
-    ext_low[...] = ext[...].astype(f32)[8 : rows + 2 * EDGE + 8].astype(bf16)
+    def halo_copies(block):
+        columns = pl.ds(block * LANES, LANES)
+        up = remote(
+            ext.at[pl.ds(EDGE, EDGE), columns],
+            ext.at[pl.ds(rows + EDGE, EDGE), columns],
+            halo_send.at[0, block],
+            halo_recv.at[1, block],
+            before,
+        )
+        down = remote(
+            ext.at[pl.ds(rows, EDGE), columns],
+            ext.at[pl.ds(0, EDGE), columns],
+            halo_send.at[1, block],
+            halo_recv.at[0, block],
+            after,
+        )
+        return up, down
+
+    halos = [halo_copies(block) for block in range(blocks + 1)]
+
+    def canvas_and_halo(block):
+        canvas_block(block * LANES, LANES)
+        pl.when(has_before)(halos[block][0].start)
+        pl.when(has_after)(halos[block][1].start)
+
+    def finish_block(block):
+        pl.when(has_before)(halos[block][1].wait_recv)
+        pl.when(has_after)(halos[block][0].wait_recv)
+        columns = slice(block * LANES, (block + 1) * LANES)
+        ext_low[:, columns] = ext[:, columns].astype(f32)[8 : rows + 2 * EDGE + 8].astype(bf16)
+
     model_rows = rows + 2 * EDGE
     wide_rows = rows + EDGE
     index = lax.broadcasted_iota(jnp.int32, (wide_rows, LANES), 0)
@@ -342,7 +333,8 @@
     inside = (index >= low_edge) & (index < high_edge)
 
     def model_block(block, squares):
-        start = pl.multiple_of(block * LANES, LANES)
+        finish_block(block + 1)
+        start = block * LANES
         window = pl.ds(start, 2 * LANES)
         parts = []
         for step in range(steps):
@@ -366,7 +358,39 @@
         difference_ref[:, pl.ds(start, LANES)] = own
         return squares + jnp.sum((own * own).reshape(rows // 8, 8, LANES), axis=0)
 
-    partial[...] = lax.fori_loop(0, blocks, model_block, jnp.zeros((8, LANES), f32))
+    ahead = 2
+    squares = jnp.zeros((8, LANES), f32)
+    for chunk in range(ahead):
+        pass_on(chunk)
+    for chunk in range(chunks):
+        if chunk + ahead < chunks:
+            pass_on(chunk + ahead)
+
+        @pl.when(has_back)
+        def _():
+            arrival(back_slot, chunk).wait_recv()
+            from_back[chunk].start()
+
+        for slot in (0, 2, 4, 6):
+            origin = me + slot - REACH
+            pl.when((origin >= 0) & (origin < devices))(arrival(slot, chunk).wait_recv)
+        for k in range(1, slot_count):
+            moved[k, pad_blocks + chunk] = jnp.dot(
+                selects[k], slots[chunk][places[k]], preferred_element_type=f32
+            )
+        if chunk >= 2:
+            canvas_and_halo(chunk - 2)
+        if chunk == 3:
+            pl.when(has_before)(sci_down.wait_recv)
+            pl.when(has_after)(sci_up.wait_recv)
+            finish_block(0)
+        if chunk >= 4:
+            squares = model_block(chunk - 4, squares)
+    for block in range(blocks - 2, blocks + 1):
+        canvas_and_halo(block)
+    for block in range(blocks - 4, blocks):
+        squares = model_block(block, squares)
+    partial[...] = squares
     part_copies = []
     for step in range(1, PIECES):
         part_copies.append(
@@ -411,8 +435,9 @@
         pl.when(has_back)(from_back[chunk].wait_send)
     pl.when(has_before)(sci_up.wait_send)
     pl.when(has_after)(sci_down.wait_send)
-    pl.when(has_before)(halo_up.wait_send)
-    pl.when(has_after)(halo_down.wait_send)
+    for up, down in halos:
+        pl.when(has_before)(up.wait_send)
+        pl.when(has_after)(down.wait_send)
     for copy in part_copies:
         copy.wait_send()
 
@@ -435,7 +460,7 @@
     psf_taps = psf_kernel.shape[0]
     f32, bf16 = jnp.float32, jnp.bfloat16
     hbm = pl.BlockSpec(memory_space=pl.ANY)
-    chunks = 4
+    chunks = 8
     slot_count = covering.shape[1]
     vmem = pl.BlockSpec(memory_space=pltpu.VMEM)
     wide = cols + LANES
@@ -478,8 +503,8 @@
             dma((2, chunks)),
             dma((2,)),
             dma((2,)),
-            dma((2,)),
-            dma((2,)),
+            dma((2, wide // LANES)),
+            dma((2, wide // LANES)),
             dma((PIECES - 1,)),
             dma((PIECES,)),
         ],

time: 46 us -> 47.7 us (1.037)
  Pallas kernels: 41.9 us -> 43.5 us
    pallas_call x1, Pallas kernels: 41.9 us -> 43.5 us  [shards(): pl.pallas_call(functools.partial(kernel, devices), out_shape=[jax.ShapeDt...]
where the time goes in v2:
time: 47.7 us; the launch traced here: 47.5 us
  Pallas kernels  43.5 us (91%)
  local copies, waits for them, and re-layouts  3.37 us (7%)
  between operations  0.65 us (1%)
    pallas_call x1, Pallas kernels, shards(): pl.pallas_call(functools.partial(kernel, devices), out_shape=[jax.ShapeDt...  43.5 us
    unnamed x4, local copies, waits for them, and re-layouts  3.37 us

profile of v2, /device:TPU:1, one launch (start us, length us, event | category | flops | bytes accessed | tf_op | source)
XLA Modules:
  0.0 47.5 jit_solution(517479634521661414)
XLA Ops:
  0.6 43.5 %shard_map.113 = (f32[256,1024]{1,0:T(8,128)}, f32[256,1024]{1,0:T(8,128)}) custom-call(s32[16]{0:T(128)} %owner_hbm.1, s32[1,4]{1,0:T(1,128)} %covering_hbm.1, s32[1,4]{1,0:T(1,128)} %row_shift_hbm.1, s32[1,4]{1,0:T(1,128)} %col_shift_hbm.1, f32[256,1024]{1,0:T(8,128)} %science_ref.1, bf16[256,1024]{1,0:T(8,128)(2,1)} %template_ref.1, ...), custom_call_target="tpu_custom_call" | custom-call | flops 4982833152 | bytes 3670016 | tf_op jit(solution)/shard_map/pallas_call | solution.py:469
  44.1 0.0 copy-start
  44.1 2.4 %copy.14 = f32[256,1024]{1,0:T(8,128)} copy(f32[256,1024]{1,0:T(8,128)} %get-tuple-element.4) | data formatting | bytes 2097152
  46.5 0.0 copy-done
  46.5 1.0 %copy.15 = f32[256,1024]{1,0:T(8,128)} copy(f32[256,1024]{1,0:T(8,128)S(1)} %copy-done) | data formatting | bytes 2097152
Async XLA Ops:
  44.1 2.4 %copy-start = (f32[256,1024]{1,0:T(8,128)S(1)}, f32[256,1024]{1,0:T(8,128)}, u32[]{:S(2)}) copy-start(f32[256,1024]{1,0:T(8,128)} %get-tuple-element.5) | copy-start | bytes 3145732

commit v3 on v1

--- a/solution.py
+++ b/solution.py
@@ -192,17 +192,15 @@
     for copy in fetches:
         copy.wait()
 
-    lane = lax.broadcasted_iota(jnp.int32, (LANES, 2 * LANES), 1)
-    tap = lax.broadcasted_iota(jnp.int32, (LANES, 2 * LANES), 0)
-    reverse = jnp.where(lax.rem(tap + lane, 2 * LANES) == 0, 1.0, 0.0).astype(bf16)
+    lane = lax.broadcasted_iota(jnp.int32, (LANES, LANES), 1)
+    line_of = lax.broadcasted_iota(jnp.int32, (LANES, LANES), 0)
+    reverse = jnp.where(lax.rem(line_of + lane, LANES) == 0, 1.0, 0.0).astype(bf16)
     small[...] = jnp.zeros_like(small)
     small[0, 0:basis, 0:taps] = basis_cols_ref[...]
     small[1, 0:basis, 0:taps] = basis_rows_ref[...]
     small[2, 0:psf_taps, 0:psf_taps] = psf_ref[...]
     small[3, 0:1, 0:basis] = coeffs_ref[pl.ds(visit, 1), :]
-    diagonal = lax.broadcasted_iota(jnp.int32, (LANES, LANES), 0) == lax.broadcasted_iota(
-        jnp.int32, (LANES, LANES), 1
-    )
+    diagonal = line_of == lane
     coeff_col = jnp.sum(
         jnp.where(diagonal, jnp.broadcast_to(small[3, 0:1, :], (LANES, LANES)), 0.0),
         axis=1,
@@ -215,23 +213,36 @@
     )
     folded[1] = jnp.dot(small[2].astype(bf16), reverse, preferred_element_type=f32)
 
-    def band(which, index):
+    lower = lane <= line_of
+
+    def band(which, index, target, start, s):
         line = folded[which, pl.ds(index, 1), :]
-        spread = jnp.broadcast_to(line, (2 * LANES, 2 * LANES))
+        spread = jnp.broadcast_to(line, (LANES, LANES))
         rolled = pltpu.roll(spread, 0, 1, stride=1, stride_axis=0)
-        return rolled[:, :LANES].astype(bf16)
+        columns = slice(s * LANES, (s + 1) * LANES)
+        target[pl.ds(start, LANES), columns] = jnp.where(lower, rolled, 0.0).astype(bf16)
+        target[pl.ds(start + LANES, LANES), columns] = jnp.where(lower, 0.0, rolled).astype(bf16)
 
     steps = (taps + 7) // 8
+    early = min(steps, chunks)
+
+    def pass_on(chunk):
+        arrival(beside_slot, chunk).wait_recv()
+        pl.when(has_onward)(to_onward[chunk].start)
+        from_beside[chunk].start()
+
 
     def build(step, carry):
+        for chunk in range(early):
+            pl.when(step == chunk)(functools.partial(pass_on, chunk))
         start = pl.multiple_of(step * (2 * LANES), 2 * LANES)
         for s in range(8):
-            weights[pl.ds(start, 2 * LANES), s * LANES : (s + 1) * LANES] = band(0, step * 8 + s)
+            band(0, step * 8 + s, weights, start, s)
         return carry
 
     lax.fori_loop(0, steps, build, 0)
     for s in range(psf_taps):
-        psf_weights[:, s * LANES : (s + 1) * LANES] = band(1, s)
+        band(1, s, psf_weights, 0, s)
 
     sci_ext[pl.ds(rows + 16, 8), :] = jnp.zeros((8, cols), f32)
     ext[pl.ds(rows + 2 * EDGE, EDGE), :] = jnp.zeros((EDGE, ext.shape[1]), bf16)
@@ -264,11 +275,6 @@
         row_offs.append(row_shift_ref[0, k])
         col_offs.append(col_shift_ref[0, k])
         selects.append(jnp.where(row_to - row_from == row_offs[k], 1.0, 0.0).astype(bf16))
-
-    def pass_on(chunk):
-        arrival(beside_slot, chunk).wait_recv()
-        pl.when(has_onward)(to_onward[chunk].start)
-        from_beside[chunk].start()
 
     def canvas_block(start, width):
         col = lax.broadcasted_iota(jnp.int32, (1, width), 1) + (start - rim)
@@ -290,10 +296,9 @@
         image = jnp.where((col >= 0) & (col < cols), total / coverage, 0.0)
         ext[pl.ds(EDGE, rows), start : start + width] = image.astype(bf16)
 
-    pass_on(0)
     for chunk in range(chunks):
-        if chunk + 1 < chunks:
-            pass_on(chunk + 1)
+        if early + chunk < chunks:
+            pass_on(early + chunk)
 
         @pl.when(has_back)
         def _():
@@ -462,7 +467,7 @@
             pltpu.VMEM((rows + 2 * EDGE, wide), bf16),
             pltpu.VMEM((rows + 24, cols), f32),
             pltpu.VMEM((4, LANES, LANES), f32),
-            pltpu.VMEM((2, LANES, 2 * LANES), f32),
+            pltpu.VMEM((2, LANES, LANES), f32),
             pltpu.VMEM((steps * 2 * LANES, 8 * LANES), bf16),
             pltpu.VMEM((2 * LANES, psf_taps * LANES), bf16),
             pltpu.VMEM((8, rows + 2 * EDGE, LANES), f32),

time: 46 us -> 45.3 us (0.985)
  Pallas kernels: 41.9 us -> 41.1 us
    pallas_call x1, Pallas kernels: 41.9 us -> 41.1 us  [shards(): pl.pallas_call(functools.partial(kernel, devices), out_shape=[jax.ShapeDt...]
where the time goes in v3:
time: 45.3 us; the launch traced here: 45.1 us
  Pallas kernels  41.1 us (91%)
  local copies, waits for them, and re-layouts  3.37 us (7%)
  between operations  0.65 us (1%)
    pallas_call x1, Pallas kernels, shards(): pl.pallas_call(functools.partial(kernel, devices), out_shape=[jax.ShapeDt...  41.1 us
    unnamed x4, local copies, waits for them, and re-layouts  3.37 us

profile of v3, /device:TPU:1, one launch (start us, length us, event | category | flops | bytes accessed | tf_op | source)
XLA Modules:
  0.0 45.1 jit_solution(16810036361059038446)
XLA Ops:
  0.6 41.1 %shard_map.113 = (f32[256,1024]{1,0:T(8,128)}, f32[256,1024]{1,0:T(8,128)}) custom-call(s32[16]{0:T(128)} %owner_hbm.1, s32[1,4]{1,0:T(1,128)} %covering_hbm.1, s32[1,4]{1,0:T(1,128)} %row_shift_hbm.1, s32[1,4]{1,0:T(1,128)} %col_shift_hbm.1, f32[256,1024]{1,0:T(8,128)} %science_ref.1, bf16[256,1024]{1,0:T(8,128)(2,1)} %template_ref.1, ...), custom_call_target="tpu_custom_call" | custom-call | flops 4982833152 | bytes 3670016 | tf_op jit(solution)/shard_map/pallas_call | solution.py:449
  41.8 0.0 copy-start
  41.8 2.4 %copy.14 = f32[256,1024]{1,0:T(8,128)} copy(f32[256,1024]{1,0:T(8,128)} %get-tuple-element.4) | data formatting | bytes 2097152
  44.2 0.0 copy-done
  44.2 1.0 %copy.15 = f32[256,1024]{1,0:T(8,128)} copy(f32[256,1024]{1,0:T(8,128)S(1)} %copy-done) | data formatting | bytes 2097152
Async XLA Ops:
  41.8 2.4 %copy-start = (f32[256,1024]{1,0:T(8,128)S(1)}, f32[256,1024]{1,0:T(8,128)}, u32[]{:S(2)}) copy-start(f32[256,1024]{1,0:T(8,128)} %get-tuple-element.5) | copy-start | bytes 3145732

commit v4 on v3

--- a/solution.py
+++ b/solution.py
@@ -26,6 +26,8 @@
     basis_rows_hbm,
     coeffs_hbm,
     psf_hbm,
+    difference_hbm,
+    detection_hbm,
     difference_ref,
     detection_ref,
     owner_ref,
@@ -66,6 +68,7 @@
     halo_recv,
     part_send,
     part_recv,
+    out_sem,
 ):
     rows, cols = science_ref.shape
     blocks = cols // LANES
@@ -296,6 +299,38 @@
         image = jnp.where((col >= 0) & (col < cols), total / coverage, 0.0)
         ext[pl.ds(EDGE, rows), start : start + width] = image.astype(bf16)
 
+    spans = [(chunk * chunk_cols, chunk_cols) for chunk in range(chunks)] + [(cols, LANES)]
+    halos = []
+    for number, (start, width) in enumerate(spans):
+        columns = pl.ds(start, width)
+        up = remote(
+            ext.at[pl.ds(EDGE, EDGE), columns],
+            ext.at[pl.ds(rows + EDGE, EDGE), columns],
+            halo_send.at[0, number],
+            halo_recv.at[1, number],
+            before,
+        )
+        down = remote(
+            ext.at[pl.ds(rows, EDGE), columns],
+            ext.at[pl.ds(0, EDGE), columns],
+            halo_send.at[1, number],
+            halo_recv.at[0, number],
+            after,
+        )
+        halos.append((up, down))
+
+    def canvas_and_halo(number):
+        canvas_block(*spans[number])
+        pl.when(has_before)(halos[number][0].start)
+        pl.when(has_after)(halos[number][1].start)
+
+    def finish_span(number):
+        pl.when(has_before)(halos[number][1].wait_recv)
+        pl.when(has_after)(halos[number][0].wait_recv)
+        start, width = spans[number]
+        columns = slice(start, start + width)
+        ext_low[:, columns] = ext[:, columns].astype(f32)[8 : rows + 2 * EDGE + 8].astype(bf16)
+
     for chunk in range(chunks):
         if early + chunk < chunks:
             pass_on(early + chunk)
@@ -315,30 +350,10 @@
                     :, part * LANES : (part + 1) * LANES
                 ]
         if chunk:
-            canvas_block((chunk - 1) * chunk_cols, chunk_cols)
-    canvas_block(cols - chunk_cols, chunk_cols)
-    canvas_block(cols, LANES)
-
-    halo_up = remote(
-        ext.at[pl.ds(EDGE, EDGE)], ext.at[pl.ds(rows + EDGE, EDGE)], halo_send.at[0], halo_recv.at[1], before
-    )
-    halo_down = remote(
-        ext.at[pl.ds(rows, EDGE)], ext.at[pl.ds(0, EDGE)], halo_send.at[1], halo_recv.at[0], after
-    )
-    pl.when(has_before)(halo_up.start)
-    pl.when(has_after)(halo_down.start)
-
-    @pl.when(has_before)
-    def _():
-        halo_down.wait_recv()
-        sci_down.wait_recv()
-
-    @pl.when(has_after)
-    def _():
-        halo_up.wait_recv()
-        sci_up.wait_recv()
-
-    ext_low[...] = ext[...].astype(f32)[8 : rows + 2 * EDGE + 8].astype(bf16)
+            canvas_and_halo(chunk - 1)
+    canvas_and_halo(chunks - 1)
+    canvas_and_halo(chunks)
+
     model_rows = rows + 2 * EDGE
     wide_rows = rows + EDGE
     index = lax.broadcasted_iota(jnp.int32, (wide_rows, LANES), 0)
@@ -371,7 +386,18 @@
         difference_ref[:, pl.ds(start, LANES)] = own
         return squares + jnp.sum((own * own).reshape(rows // 8, 8, LANES), axis=0)
 
-    partial[...] = lax.fori_loop(0, blocks, model_block, jnp.zeros((8, LANES), f32))
+    pl.when(has_before)(sci_down.wait_recv)
+    pl.when(has_after)(sci_up.wait_recv)
+    ready = chunks // 2
+    for number in range(ready):
+        finish_span(number)
+    first_blocks = ready * chunk_cols // LANES - 1
+    squares = lax.fori_loop(0, first_blocks, model_block, jnp.zeros((8, LANES), f32))
+    for number in range(ready, chunks + 1):
+        finish_span(number)
+    partial[...] = lax.fori_loop(first_blocks, blocks, model_block, squares)
+    difference_copy = pltpu.make_async_copy(difference_ref, difference_hbm, out_sem.at[0])
+    difference_copy.start()
     part_copies = []
     for step in range(1, PIECES):
         part_copies.append(
@@ -406,6 +432,8 @@
         ).wait_recv()
     variance = jnp.sum(jnp.sum(partials[...], axis=0), keepdims=True) / (PIECES * rows * cols)
     detection_ref[...] = detection_ref[...] / jnp.sqrt(variance + 1e-06)
+    detection_copy = pltpu.make_async_copy(detection_ref, detection_hbm, out_sem.at[1])
+    detection_copy.start()
 
     for chunk in range(chunks):
         to_beside[chunk].wait_send()
@@ -416,10 +444,27 @@
         pl.when(has_back)(from_back[chunk].wait_send)
     pl.when(has_before)(sci_up.wait_send)
     pl.when(has_after)(sci_down.wait_send)
-    pl.when(has_before)(halo_up.wait_send)
-    pl.when(has_after)(halo_down.wait_send)
+    for up, down in halos:
+        pl.when(has_before)(up.wait_send)
+        pl.when(has_after)(down.wait_send)
+    difference_copy.wait()
+    detection_copy.wait()
     for copy in part_copies:
         copy.wait_send()
+
+
+def hand_out(difference, detection, difference_out, detection_out, sem):
+    parts = sem.shape[1]
+    size = difference.shape[0] // parts
+    copies = []
+    for number, (src, dst) in enumerate(((difference, difference_out), (detection, detection_out))):
+        for part in range(parts):
+            span = pl.ds(part * size, size)
+            copies.append(pltpu.make_async_copy(src.at[span], dst.at[span], sem.at[number, part]))
+    for copy in copies:
+        copy.start()
+    for copy in copies:
+        copy.wait()
 
 
 def shards(
@@ -442,16 +487,17 @@
     hbm = pl.BlockSpec(memory_space=pl.ANY)
     chunks = 4
     slot_count = covering.shape[1]
-    vmem = pl.BlockSpec(memory_space=pltpu.VMEM)
     wide = cols + LANES
     dma = pltpu.SemaphoreType.DMA
     flops = 2 * cols * (rows + 32) * (2 * LANES) * (8 * steps + psf_taps)
-    return pl.pallas_call(
+    results = pl.pallas_call(
         functools.partial(kernel, devices),
         out_shape=[jax.ShapeDtypeStruct((rows, cols), f32)] * 2,
         in_specs=[hbm] * 10,
-        out_specs=[vmem] * 2,
+        out_specs=[hbm] * 2,
         scratch_shapes=[
+            pltpu.VMEM((rows, cols), f32),
+            pltpu.VMEM((rows, cols), f32),
             pltpu.SMEM(owner_map.shape, jnp.int32),
             pltpu.SMEM(covering.shape, jnp.int32),
             pltpu.SMEM(row_shift.shape, jnp.int32),
@@ -483,10 +529,11 @@
             dma((2, chunks)),
             dma((2,)),
             dma((2,)),
-            dma((2,)),
-            dma((2,)),
+            dma((2, chunks + 1)),
+            dma((2, chunks + 1)),
             dma((PIECES - 1,)),
             dma((PIECES,)),
+            dma((2,)),
         ],
         compiler_params=pltpu.CompilerParams(
             collective_id=0, has_side_effects=True, vmem_limit_bytes=60 * 1024 * 1024
@@ -506,6 +553,15 @@
         coeffs,
         psf_kernel,
     )
+    return pl.pallas_call(
+        hand_out,
+        out_shape=[jax.ShapeDtypeStruct((rows, cols), f32)] * 2,
+        in_specs=[hbm] * 2,
+        out_specs=[hbm] * 2,
+        scratch_shapes=[dma((2, 4))],
+        compiler_params=pltpu.CompilerParams(vmem_limit_bytes=60 * 1024 * 1024),
+        cost_estimate=pl.CostEstimate(flops=0, bytes_accessed=rows * cols * 16, transcendentals=0),
+    )(*results)
 
 
 def solution(mesh):

time: 45.3 us -> 104 us (2.30)
  Pallas kernels: 41.1 us -> 104 us
  local copies, waits for them, and re-layouts: 3.37 us -> 0 us
    pallas_call x0 -> x1, Pallas kernels: none -> 64.7 us  [shards(): pl.pallas_call(hand_out, out_shape=[jax.ShapeDtypeStruct((rows, cols), f3...]
    unnamed x4 -> x0, local copies, waits for them, and re-layouts: 3.37 us -> none
    pallas_call x1, Pallas kernels: 41.1 us -> 38.8 us  [shards(): pl.pallas_call(functools.partial(kernel, devices), out_shape=[jax.ShapeDt...]
where the time goes in v4:
time: 104 us
  Pallas kernels  104 us (100%)
    pallas_call x1, Pallas kernels, shards(): pl.pallas_call(hand_out, out_shape=[jax.ShapeDtypeStruct((rows, cols), f3...  64.7 us
    pallas_call x1, Pallas kernels, shards(): pl.pallas_call(functools.partial(kernel, devices), out_shape=[jax.ShapeDt...  38.8 us

profile of v4, /device:TPU:1, one launch (start us, length us, event | category | flops | bytes accessed | tf_op | source)
XLA Modules:
  0.0 104.2 jit_solution(16325981832698832736)
XLA Ops:
  0.6 38.8 %shard_map.113 = (f32[256,1024]{1,0:T(8,128)}, f32[256,1024]{1,0:T(8,128)}) custom-call(s32[16]{0:T(128)} %owner_hbm.1, s32[1,4]{1,0:T(1,128)} %covering_hbm.1, s32[1,4]{1,0:T(1,128)} %row_shift_hbm.1, s32[1,4]{1,0:T(1,128)} %col_shift_hbm.1, f32[256,1024]{1,0:T(8,128)} %science_ref.1, bf16[256,1024]{1,0:T(8,128)(2,1)} %template_ref.1, ...), custom_call_target="tpu_custom_call" | custom-call | flops 4982833152 | bytes 3670016 | tf_op jit(solution)/shard_map/pallas_call | solution.py:493
  39.5 64.7 %shard_map.114 = (f32[256,1024]{1,0:T(8,128)}, f32[256,1024]{1,0:T(8,128)}) custom-call(f32[256,1024]{1,0:T(8,128)} %get-tuple-element.4.difference, f32[256,1024]{1,0:T(8,128)} %get-tuple-element.5.detection), custom_call_target="tpu_custom_call" | custom-call | bytes 4194304 | tf_op jit(solution)/shard_map/pallas_call | solution.py:556

commit v5 on v4

--- a/solution.py
+++ b/solution.py
@@ -453,18 +453,9 @@
         copy.wait_send()
 
 
-def hand_out(difference, detection, difference_out, detection_out, sem):
-    parts = sem.shape[1]
-    size = difference.shape[0] // parts
-    copies = []
-    for number, (src, dst) in enumerate(((difference, difference_out), (detection, detection_out))):
-        for part in range(parts):
-            span = pl.ds(part * size, size)
-            copies.append(pltpu.make_async_copy(src.at[span], dst.at[span], sem.at[number, part]))
-    for copy in copies:
-        copy.start()
-    for copy in copies:
-        copy.wait()
+def hand_out(difference, detection, difference_out, detection_out):
+    difference_out[...] = difference[...]
+    detection_out[...] = detection[...]
 
 
 def shards(
@@ -553,12 +544,13 @@
         coeffs,
         psf_kernel,
     )
+    block = pl.BlockSpec((rows // 4, cols), lambda step: (step, 0))
     return pl.pallas_call(
         hand_out,
+        grid=(4,),
         out_shape=[jax.ShapeDtypeStruct((rows, cols), f32)] * 2,
-        in_specs=[hbm] * 2,
-        out_specs=[hbm] * 2,
-        scratch_shapes=[dma((2, 4))],
+        in_specs=[block] * 2,
+        out_specs=[block] * 2,
         compiler_params=pltpu.CompilerParams(vmem_limit_bytes=60 * 1024 * 1024),
         cost_estimate=pl.CostEstimate(flops=0, bytes_accessed=rows * cols * 16, transcendentals=0),
     )(*results)

time: 104 us -> 43.4 us (0.42)
  Pallas kernels: 104 us -> 42.6 us
    pallas_call x1, Pallas kernels: 64.7 us -> 3.75 us  [shards(): pl.pallas_call(hand_out, grid=(4,), out_shape=[jax.ShapeDtypeStruct((rows...]
where the time goes in v5:
time: 43.4 us; the launch traced here: 43.2 us
  Pallas kernels  42.6 us (98%)
  between operations  0.64 us (1%)
    pallas_call x1, Pallas kernels, shards(): pl.pallas_call(functools.partial(kernel, devices), out_shape=[jax.ShapeDt...  38.8 us
    pallas_call x1, Pallas kernels, shards(): pl.pallas_call(hand_out, grid=(4,), out_shape=[jax.ShapeDtypeStruct((rows...  3.75 us

profile of v5, /device:TPU:1, one launch (start us, length us, event | category | flops | bytes accessed | tf_op | source)
XLA Modules:
  0.0 43.2 jit_solution(6333076720816591113)
XLA Ops:
  0.6 38.8 %shard_map.113 = (f32[256,1024]{1,0:T(8,128)}, f32[256,1024]{1,0:T(8,128)}) custom-call(s32[16]{0:T(128)} %owner_hbm.1, s32[1,4]{1,0:T(1,128)} %covering_hbm.1, s32[1,4]{1,0:T(1,128)} %row_shift_hbm.1, s32[1,4]{1,0:T(1,128)} %col_shift_hbm.1, f32[256,1024]{1,0:T(8,128)} %science_ref.1, bf16[256,1024]{1,0:T(8,128)(2,1)} %template_ref.1, ...), custom_call_target="tpu_custom_call" | custom-call | flops 4982833152 | bytes 3670016 | tf_op jit(solution)/shard_map/pallas_call | solution.py:484
  39.5 3.8 %shard_map.114 = (f32[256,1024]{1,0:T(8,128)}, f32[256,1024]{1,0:T(8,128)}) custom-call(f32[256,1024]{1,0:T(8,128)} %get-tuple-element.4.difference, f32[256,1024]{1,0:T(8,128)} %get-tuple-element.5.detection), custom_call_target="tpu_custom_call" | custom-call | bytes 4194304 | tf_op jit(solution)/shard_map/pallas_call | solution.py:548
